TPU v7x, 512 devices: a whole 4x8x8 slice. The times are simulated.
512 devices in a mesh: dp: 32 (over z, x_hi, core), clus: 16 (over x_lo, y).
Axes of the slice: x: 4 (x_hi: 2, x_lo: 2; x = x_hi * 2 + x_lo), y: 8, z: 8, core: 2. Of those that a mesh axis runs over, the one named last changes fastest.
Arguments:
- rows: bfloat16 [131072, 1024], P(('dp', 'clus')), may hold values from -8 to 8
- fine_assign: int32 [131072], P(('dp', 'clus')), may hold values from 0 to 131071, as said below
- parent1: int32 [131072], P(('dp', 'clus')), may hold values from 0 to 8191, as said below
- parent2: int32 [8192], P('dp'), may hold values from 0 to 511
- parent3: int32 [512], replicated, may hold values from 0 to 63
- shrink: float32 [4], replicated, may hold values from 0.5 to 2
Outputs:
- fine_centroids: bfloat16 [131072, 1024], P(('dp', 'clus'))
- mid_centroids: bfloat16 [8192, 1024], P(('dp', 'clus'))
- coarse_centroids: bfloat16 [512, 1024], P(('dp', 'clus'))
- spread: float32 [131072], P(('dp', 'clus'))
Inputs may be any that keep to these rules, and one draw needn't show every extreme that they name: `fine_assign`: devices are numbered d = dp index * 16 + clus index, and fine centroid k is owned by device k // 256. Every row of device d names a fine centroid owned by a device of the same dp index. At most 32 rows of one device name centroids of one owner, and in every dp group some owner is named by exactly 32 rows of each device of the group. parent1[k] is one of the 256 second-level centroids g * 256 to g * 256 + 255, with g = k // 4096.
All inputs are finite; a program needn't handle non-finite values.
Results may differ from a plain program's by a relative error of at most 0.0035.
Values may be sent and summed in bfloat16 or wider, within the bound.
No kernel may reach another device: no remote copies, remote signals or barrier semaphores. Data moves between devices by JAX's collectives and lax.ppermute only.
A program may use at most 64 MiB of HBM per device.

v0:
```python
import math
import jax
import jax.numpy as jnp
from jax import lax
from jax.sharding import PartitionSpec as P

K4 = 64
HIGH = lax.Precision.HIGHEST


def split_up(x, dim, count):
    shape = x.shape
    parts = x.reshape(*shape[:dim], count, shape[dim] // count, *shape[dim + 1 :])
    return jnp.moveaxis(parts, dim, 0)


def sent_and_summed(x, axis, dim):
    parts = split_up(x, dim, lax.axis_size(axis))
    arrived = lax.all_to_all(parts, axis, split_axis=0, concat_axis=0, tiled=True)
    return arrived.sum(axis=0)


def in_one_piece(arrays, axis, dim, along):
    widths = [math.prod(a.shape[along:]) for a in arrays]
    both = jnp.concatenate(
        [a.reshape(*a.shape[:along], w) for a, w in zip(arrays, widths)], axis=along
    )
    whole = sent_and_summed(both, axis, dim)
    parts = jnp.split(whole, [sum(widths[:k]) for k in range(1, len(widths))], axis=along)
    return tuple((b.reshape(*whole.shape[:along], *a.shape[along:]) for a, b in zip(arrays, parts)))


def in_order(parts, dim):
    shape = list(parts.shape[1:])
    shape[dim] *= parts.shape[0]
    return jnp.moveaxis(parts, 0, dim).reshape(shape)


def copy_for_each(x, axis):
    copies = jnp.broadcast_to(x, (lax.axis_size(axis), *x.shape))
    return lax.all_to_all(copies, axis, split_axis=0, concat_axis=0, tiled=True)


def collect(x, axis, dim):
    return in_order(copy_for_each(x, axis), dim)


def shrunk(sums, counts, prior, weight):
    return (sums + weight * prior) / (counts + weight)[:, None]


def local(rows, fine_assign, parent1, parent2, parent3, shrink):
    groups = lax.axis_size("clus")
    dp_count = lax.axis_size("dp")
    devices = groups * dp_count
    clus_index = lax.axis_index("clus")
    dp_index = lax.axis_index("dp")
    count = rows.shape[0]
    width = rows.shape[1]
    fine_dev = parent1.shape[0]
    middle_dp = parent2.shape[0]
    third = parent3.shape[0]
    slots = 2 * count // groups
    total = count * devices
    weight_top = shrink[0] * (total / K4)
    weight_third = shrink[1] * (total / third)
    weight_middle = shrink[2] * (total / (middle_dp * dp_count))
    weight_fine = shrink[3] * (total / (fine_dev * devices))
    local_ids = fine_assign - dp_index * groups * fine_dev
    target = local_ids // fine_dev
    within = local_ids - target * fine_dev
    target_hot = (target[:, None] == jnp.arange(groups)[None, :]).astype(jnp.bfloat16)
    earlier = (jnp.arange(count)[:, None] > jnp.arange(count)[None, :]).astype(jnp.bfloat16)
    before = jnp.dot(earlier, target_hot, preferred_element_type=jnp.float32)
    rank = jnp.sum(before * target_hot.astype(jnp.float32), axis=1).astype(jnp.int32)
    slot_of = target * slots + rank
    source = (
        jnp.full((groups * slots,), count, jnp.int32)
        .at[slot_of]
        .set(jnp.arange(count, dtype=jnp.int32))
    )
    padded = jnp.concatenate([rows, jnp.zeros((1, width), jnp.bfloat16)], axis=0)
    send_rows = padded[source].reshape(groups, slots, width)
    send_ids = jnp.concatenate([within, jnp.full((1,), -1, jnp.int32)])[source].reshape(
        groups, slots
    )
    got_rows, got_ids = (
        lax.all_to_all(send_rows, "clus", split_axis=0, concat_axis=0, tiled=True),
        lax.all_to_all(send_ids, "clus", split_axis=0, concat_axis=0, tiled=True),
    )
    got_rows = got_rows.reshape(groups * slots, width)
    got_ids = got_ids.reshape(groups * slots)
    member = (got_ids[:, None] == jnp.arange(fine_dev)[None, :]).astype(jnp.bfloat16)
    contract = (((0,), (0,)), ((), ()))
    fine_sums = lax.dot_general(member, got_rows, contract, preferred_element_type=jnp.float32)
    fine_counts = jnp.sum(member.astype(jnp.float32), axis=0)
    middle_local = parent1 - dp_index * middle_dp
    child_hot = (jnp.arange(middle_dp)[:, None] == middle_local[None, :]).astype(jnp.float32)
    middle_part = jnp.dot(child_hot, fine_sums, precision=HIGH)
    middle_tally = jnp.dot(child_hot, fine_counts, precision=HIGH)
    share = middle_dp // groups
    offset = clus_index * share
    middle_sums, middle_counts = in_one_piece((middle_part, middle_tally), "clus", 0, 1)
    own_parent2 = lax.dynamic_slice_in_dim(parent2, offset, share, 0)
    third_share = third // devices
    third_start = (dp_index * groups + clus_index) * third_share
    third_hot = (jnp.arange(third)[:, None] == own_parent2[None, :]).astype(jnp.float32)
    third_part = jnp.dot(third_hot, middle_sums, precision=HIGH)
    third_tally = jnp.dot(third_hot, middle_counts, precision=HIGH)
    third_sums, third_counts = lax.psum((third_part, third_tally), ("dp", "clus"))
    top_hot = (jnp.arange(K4)[:, None] == parent3[None, :]).astype(jnp.float32)
    top_sums = jnp.dot(top_hot, third_sums, precision=HIGH)
    top_counts = jnp.dot(top_hot, third_counts, precision=HIGH)
    center = jnp.sum(top_sums, axis=0) / total
    top_means = shrunk(top_sums, top_counts, center[None, :], weight_top)
    third_means = shrunk(
        third_sums, third_counts, jnp.dot(top_hot.T, top_means, precision=HIGH), weight_third
    )
    third_out = lax.dynamic_slice_in_dim(third_means, third_start, third_share, 0)
    parent_hot = (own_parent2[:, None] == jnp.arange(third)[None, :]).astype(jnp.float32)
    middle_out = shrunk(
        middle_sums, middle_counts, jnp.dot(parent_hot, third_means, precision=HIGH), weight_middle
    )
    middle_means = collect(middle_out, "clus", 0)
    fine_means = shrunk(
        fine_sums, fine_counts, jnp.dot(child_hot.T, middle_means, precision=HIGH), weight_fine
    )
    fine_out = fine_means.astype(jnp.bfloat16)
    back = jnp.dot(member, fine_out, preferred_element_type=jnp.float32)
    diff = got_rows.astype(jnp.float32) - back
    row_error = jnp.sum(diff * diff, axis=1)
    spread = jnp.sum(member.astype(jnp.float32) * row_error[:, None], axis=0) / (
        width * (fine_counts + 1.0)
    )
    return (fine_out, middle_out.astype(jnp.bfloat16), third_out.astype(jnp.bfloat16), spread)


def solution(mesh):
    placed = (P(("dp", "clus"), None), P(("dp", "clus")), P(("dp", "clus")), P("dp"), P(), P())
    return jax.shard_map(
        local,
        mesh=mesh,
        in_specs=placed,
        out_specs=(
            P(("dp", "clus"), None),
            P(("dp", "clus"), None),
            P(("dp", "clus"), None),
            P(("dp", "clus")),
        ),
        check_vma=False,
    )
```

profile of v0, /device:TPU:8, one launch (start us, length us, event | category | flops | bytes accessed | tf_op | source)
XLA Modules:
  0.0 429.1 jit_solution(13146403856222873392)
XLA Ops:
  7.2 0.0 copy-start.2
  7.2 0.7 multiply_subtract_fusion
  7.9 0.2 fusion.5
  8.2 1.4 scatter_custom_fusion
  9.6 3.5 gather_fusion
  13.1 0.7 all_to_all.15
  13.8 9.1 %all-to-all-start = ((s32[16,1,32]{2,1,0:T(1,128)}), s32[16,1,32]{2,1,0:T(1,128)S(1)}, u32[]{:S(2)}, u32[]{:S(2)}) async-start(s32[16,1,32]{2,1,0:T(1,128)} %all_to_all.15), calls=%async_computation | async-start | bytes 16384 | tf_op jit(solution)/shard_map/all_to_all | solution.py:89
  22.9 0.0 copy-done.2
  22.9 2.8 gather_fusion.1
  25.7 0.0 copy-start.5
  25.7 4.3 all-to-all-done
  30.0 4.9 %all-to-all-start.1 = ((bf16[16,32,1024]{2,1,0:T(8,128)(2,1)}), bf16[16,32,1024]{2,1,0:T(8,128)(2,1)S(1)}, u32[]{:S(2)}, u32[]{:S(2)}) async-start(bf16[16,32,1024]{2,1,0:T(8,128)(2,1)} %bitcast), calls=%async_computation.1 | async-start | bytes 2097152 | tf_op jit(solution)/shard_map/all_to_all | solution.py:88
  34.9 0.0 copy-done.5
  34.9 0.5 broadcast.74
  35.4 0.7 reduce.7
  36.1 0.1 eq.90
  36.2 0.2 convert_reduce_fusion
  36.3 0.3 convolution_bitcast_fusion
  36.6 22.8 %all-to-all-done.1 = bf16[16,32,1024]{2,1,0:T(8,128)(2,1)S(1)} async-done(((bf16[16,32,1024]{2,1,0:T(8,128)(2,1)}), bf16[16,32,1024]{2,1,0:T(8,128)(2,1)S(1)}, u32[]{:S(2)}, u32[]{:S(2)}) %all-to-all-start.1) | async-done | bytes 1048608 | tf_op jit(solution)/shard_map/all_to_all | solution.py:88
  59.4 0.6 fusion.9
  60.0 0.7 fusion.14
  60.7 0.0 copy-start.6
  60.7 1.1 pad_maximum_fusion
  61.9 5.2 %all-to-all-start.2 = ((f32[16,16,1025]{2,1,0:T(8,128)}), f32[16,16,1025]{2,1,0:T(8,128)S(1)}, u32[]{:S(2)}, u32[]{:S(2)}) async-start(f32[16,16,1025]{2,1,0:T(8,128)} %pad_maximum_fusion), calls=%async_computation.2 | async-start | bytes 2359296 | tf_op jit(solution)/shard_map/all_to_all | solution.py:19
  67.0 0.0 all-reduce.3.cloned.1.call-start
  67.1 0.0 copy-done.6
  67.1 0.1 dynamic_slice.6
  67.2 26.9 %all-to-all-done.2 = f32[16,16,1025]{2,1,0:T(8,128)S(1)} async-done(((f32[16,16,1025]{2,1,0:T(8,128)}), f32[16,16,1025]{2,1,0:T(8,128)S(1)}, u32[]{:S(2)}, u32[]{:S(2)}) %all-to-all-start.2) | async-done | bytes 1049632 | tf_op jit(solution)/shard_map/all_to_all | solution.py:19
  94.1 0.1 reduce_sum.56
  94.1 0.0 copy-start.3
  94.1 0.0 copy-start.4
  94.2 2.3 fusion.13
  96.4 0.0 all-reduce.3.cloned.1.call-update
  96.4 0.0 copy-done.3
  96.4 0.6 fusion.37
  99.6 0.1 add_reduce_fusion
  99.8 0.2 fusion.12
  100.0 103.9 %psum.15 = f32[512]{0:T(512)S(1)} all-reduce(f32[512]{0:T(512)S(1)} %bitcast.38), channel_id=1, replica_groups=mesh['dp'=32,'clus'=16] {'dp','clus'}, use_global_device_ids=true, to_apply=%region_6.7 | all-reduce | flops 512 | bytes 4096 | tf_op jit(solution)/shard_map/psum | solution.py:110
  203.9 0.0 copy-done.4
  203.9 0.1 fusion.6
  204.1 174.4 %all-reduce.3.cloned.1.call-done = f32[512,1024]{1,0:T(8,128)} async-done(((f32[512,1024]{1,0:T(8,128)}), f32[512,1024]{1,0:T(8,128)}) %all-reduce.3.cloned.1.call-update) | async-done | bytes 2097168 | tf_op jit(solution)/shard_map/psum | solution.py:110
  378.5 0.0 copy-start.1
  378.5 2.7 fusion.38
  381.2 0.0 copy-done.1
  381.2 1.2 add_divide_fusion
  382.4 0.0 copy-start
  382.4 1.3 copy-done
  383.7 1.4 fusion.39
  385.1 1.1 broadcast_in_dim.11
  386.2 7.9 %all-to-all-start.3 = ((f32[16,16,1024]{2,1,0:T(8,128)}), f32[16,16,1024]{2,1,0:T(8,128)S(1)}, u32[]{:S(2)}, u32[]{:S(2)}) async-start(f32[16,16,1024]{2,1,0:T(8,128)} %broadcast_in_dim.11), calls=%async_computation.3 | async-start | bytes 2097152 | tf_op jit(solution)/shard_map/all_to_all | solution.py:41
  394.1 0.6 broadcast_add_fusion.1
  394.8 1.4 dynamic-slice_convert_fusion
  396.2 23.3 %all-to-all-done.3 = f32[16,16,1024]{2,1,0:T(8,128)S(1)} async-done(((f32[16,16,1024]{2,1,0:T(8,128)}), f32[16,16,1024]{2,1,0:T(8,128)S(1)}, u32[]{:S(2)}, u32[]{:S(2)}) %all-to-all-start.3) | async-done | bytes 1048608 | tf_op jit(solution)/shard_map/all_to_all | solution.py:41
  419.4 1.4 fusion.2
  420.8 0.0 copy-start.7
  420.9 0.6 multiply_reduce_fusion
  421.4 0.2 fusion.7
  421.6 0.6 multiply_divide_fusion
  422.2 0.0 copy-done.7
  (10 shorter events, 0.1 us)
Async XLA Ops:
  7.2 15.7 %copy-start.2 = (bf16[256,1024]{1,0:T(8,128)(2,1)S(1)}, bf16[256,1024]{1,0:T(8,128)(2,1)}, u32[]{:S(2)}) copy-start(bf16[256,1024]{1,0:T(8,128)(2,1)} %param.6) | copy-start | bytes 1572868
  13.8 16.2 %all-to-all-start = ((s32[16,1,32]{2,1,0:T(1,128)}), s32[16,1,32]{2,1,0:T(1,128)S(1)}, u32[]{:S(2)}, u32[]{:S(2)}) async-start(s32[16,1,32]{2,1,0:T(1,128)} %all_to_all.15), calls=%async_computation | async-start | bytes 16384 | tf_op jit(solution)/shard_map/all_to_all | solution.py:89
  25.7 9.2 %copy-start.5 = (s32[256]{0:T(256)S(1)}, s32[256]{0:T(256)}, u32[]{:S(2)}) copy-start(s32[256]{0:T(256)} %param.8) | copy-start | bytes 3076
  30.0 29.5 %all-to-all-start.1 = ((bf16[16,32,1024]{2,1,0:T(8,128)(2,1)}), bf16[16,32,1024]{2,1,0:T(8,128)(2,1)S(1)}, u32[]{:S(2)}, u32[]{:S(2)}) async-start(bf16[16,32,1024]{2,1,0:T(8,128)(2,1)} %bitcast), calls=%async_computation.1 | async-start | bytes 2097152 | tf_op jit(solution)/shard_map/all_to_all | solution.py:88
  60.7 6.3 %copy-start.6 = (s32[256]{0:T(256)S(1)}, s32[256]{0:T(256)}, u32[]{:S(2)}) copy-start(s32[256]{0:T(256)} %param.9) | copy-start | bytes 3076
  61.9 32.2 %all-to-all-start.2 = ((f32[16,16,1025]{2,1,0:T(8,128)}), f32[16,16,1025]{2,1,0:T(8,128)S(1)}, u32[]{:S(2)}, u32[]{:S(2)}) async-start(f32[16,16,1025]{2,1,0:T(8,128)} %pad_maximum_fusion), calls=%async_computation.2 | async-start | bytes 2359296 | tf_op jit(solution)/shard_map/all_to_all | solution.py:19
  67.0 311.4 %all-reduce.3.cloned.1.call-start = ((), (), s32[]{:S(2)}) async-start(), calls=%async_computation.4 | async-start | bytes 4194304 | tf_op jit(solution)/shard_map/psum | solution.py:110
  94.1 2.3 copy-start.3
  94.1 109.8 %copy-start.4 = (s32[512]{0:T(512)S(1)}, s32[512]{0:T(512)}, u32[]{:S(2)}) copy-start(s32[512]{0:T(512)} %param.10) | copy-start | bytes 6148
  378.5 2.7 copy-start.1
  382.4 1.4 copy-start
  386.2 33.2 %all-to-all-start.3 = ((f32[16,16,1024]{2,1,0:T(8,128)}), f32[16,16,1024]{2,1,0:T(8,128)S(1)}, u32[]{:S(2)}, u32[]{:S(2)}) async-start(f32[16,16,1024]{2,1,0:T(8,128)} %broadcast_in_dim.11), calls=%async_computation.3 | async-start | bytes 2097152 | tf_op jit(solution)/shard_map/all_to_all | solution.py:41
  420.8 1.4 copy-start.7
Sparse Core Ops, SparseCore 0:
  96.6 281.8 all-reduce.2
where the time goes:
time: 430 us; the launch traced here: 429 us
  waiting for transfers between devices  252 us (59%)
  blocking collectives  104 us (24%)
  starting transfers between devices  27.1 us (6%)
  between operations  16.9 us (4%)
  local copies, waits for them, and re-layouts  13.5 us (3%)
  matrix products  11.6 us (3%)
  other arithmetic  4.36 us (1%)
    psum x1, waiting for transfers between devices, local(): lax.psum((third_part, third_tally), ('dp', 'clus'))  174 us
    psum x1, blocking collectives, local(): lax.psum((third_part, third_tally), ('dp', 'clus'))  104 us
    all_to_all x1, waiting for transfers between devices, sent_and_summed(): lax.all_to_all(parts, axis, split_axis=0, concat_axis=0, tiled=True)  26.9 us
    all_to_all x1, waiting for transfers between devices, copy_for_each(): return lax.all_to_all(copies, axis, split_axis=0, concat_axis=0, tiled=True)  23.3 us
    all_to_all x1, waiting for transfers between devices, local(): lax.all_to_all(send_rows, 'clus', split_axis=0, concat_axis=0, tiled=True)  22.8 us
    all_to_all x1, starting transfers between devices, local(): lax.all_to_all(send_ids, 'clus', split_axis=0, concat_axis=0, tiled=True)  9.08 us
  transfers between devices with their start and end apart: 5, of which 5 were waited for; matrix products, arithmetic and copies ran while one was open for 2% of the time, Pallas kernels for 0%

commit v1 on v0

--- a/solution.py
+++ b/solution.py
@@ -107,7 +107,7 @@
     third_hot = (jnp.arange(third)[:, None] == own_parent2[None, :]).astype(jnp.float32)
     third_part = jnp.dot(third_hot, middle_sums, precision=HIGH)
     third_tally = jnp.dot(third_hot, middle_counts, precision=HIGH)
-    third_sums, third_counts = lax.psum((third_part, third_tally), ("dp", "clus"))
+    third_sums, third_counts = lax.psum(lax.psum((third_part, third_tally), "clus"), "dp")
     top_hot = (jnp.arange(K4)[:, None] == parent3[None, :]).astype(jnp.float32)
     top_sums = jnp.dot(top_hot, third_sums, precision=HIGH)
     top_counts = jnp.dot(top_hot, third_counts, precision=HIGH)

time: 430 us -> 579 us (1.35)
  waiting for transfers between devices: 252 us -> 408 us
  blocking collectives: 104 us -> 97.3 us
    psum x1 -> x2, waiting for transfers between devices: 174 us -> 329 us  [the longest x1 180 us: local(): lax.psum(lax.psum((third_part, third_tally), 'clus'), 'dp')]
    psum x1 -> x2, blocking collectives: 104 us -> 97.3 us  [the longest x1 65.4 us: local(): lax.psum(lax.psum((third_part, third_tally), 'clus'), 'dp')]
  transfers between devices with their start and end apart: 5 -> 6, of which waited for: 5 -> 6; matrix products, arithmetic and copies ran while one was open for 2% -> 1% of each run, Pallas kernels for 0% -> 0%
where the time goes in v1:
time: 579 us; the launch traced here: 578 us
  waiting for transfers between devices  408 us (70%)
  blocking collectives  97.3 us (17%)
  starting transfers between devices  26.6 us (5%)
  between operations  16.9 us (3%)
  local copies, waits for them, and re-layouts  13.5 us (2%)
  matrix products  11.6 us (2%)
    psum x1, waiting for transfers between devices, local(): lax.psum(lax.psum((third_part, third_tally), 'clus'), 'dp')  180 us
    psum x1, waiting for transfers between devices, local(): lax.psum((third_part, third_tally), 'clus')  149 us
    psum x1, blocking collectives, local(): lax.psum(lax.psum((third_part, third_tally), 'clus'), 'dp')  65.4 us
    psum x1, blocking collectives, local(): lax.psum((third_part, third_tally), 'clus')  31.9 us
    all_to_all x1, waiting for transfers between devices, sent_and_summed(): lax.all_to_all(parts, axis, split_axis=0, concat_axis=0, tiled=True)  26.9 us
    all_to_all x1, waiting for transfers between devices, copy_for_each(): return lax.all_to_all(copies, axis, split_axis=0, concat_axis=0, tiled=True)  24.9 us
    all_to_all x1, waiting for transfers between devices, local(): lax.all_to_all(send_rows, 'clus', split_axis=0, concat_axis=0, tiled=True)  22.8 us
  transfers between devices with their start and end apart: 6, of which 6 were waited for; matrix products, arithmetic and copies ran while one was open for 1% of the time, Pallas kernels for 0%

profile of v1, /device:TPU:8, one launch (start us, length us, event | category | flops | bytes accessed | tf_op | source)
XLA Modules:
  0.0 578.4 jit_solution(13971153242026515792)
XLA Ops:
  7.2 0.0 copy-start.2
  7.2 0.7 multiply_subtract_fusion
  7.9 0.2 fusion.5
  8.2 1.4 scatter_custom_fusion
  9.6 3.5 gather_fusion
  13.1 0.7 all_to_all.15
  13.8 9.1 %all-to-all-start = ((s32[16,1,32]{2,1,0:T(1,128)}), s32[16,1,32]{2,1,0:T(1,128)S(1)}, u32[]{:S(2)}, u32[]{:S(2)}) async-start(s32[16,1,32]{2,1,0:T(1,128)} %all_to_all.15), calls=%async_computation | async-start | bytes 16384 | tf_op jit(solution)/shard_map/all_to_all | solution.py:89
  22.9 0.0 copy-done.2
  22.9 2.8 gather_fusion.1
  25.7 0.0 copy-start.5
  25.7 4.3 all-to-all-done
  30.0 4.9 all-to-all-start.1
  34.9 0.0 copy-done.5
  34.9 0.5 broadcast.74
  35.4 0.7 reduce.7
  36.1 0.1 eq.90
  36.2 0.2 convert_reduce_fusion
  36.3 0.3 convolution_bitcast_fusion
  36.6 22.8 %all-to-all-done.1 = bf16[16,32,1024]{2,1,0:T(8,128)(2,1)S(1)} async-done(((bf16[16,32,1024]{2,1,0:T(8,128)(2,1)}), bf16[16,32,1024]{2,1,0:T(8,128)(2,1)S(1)}, u32[]{:S(2)}, u32[]{:S(2)}) %all-to-all-start.1) | async-done | bytes 1048608 | tf_op jit(solution)/shard_map/all_to_all | solution.py:88
  59.4 0.6 fusion.9
  60.0 0.7 fusion.14
  60.7 0.0 copy-start.6
  60.7 1.1 pad_maximum_fusion
  61.9 5.2 all-to-all-start.2
  67.0 0.0 all-reduce.4.cloned.1.call-start
  67.1 0.0 copy-done.6
  67.1 0.1 dynamic_slice.6
  67.2 26.9 %all-to-all-done.2 = f32[16,16,1025]{2,1,0:T(8,128)S(1)} async-done(((f32[16,16,1025]{2,1,0:T(8,128)}), f32[16,16,1025]{2,1,0:T(8,128)S(1)}, u32[]{:S(2)}, u32[]{:S(2)}) %all-to-all-start.2) | async-done | bytes 1049632 | tf_op jit(solution)/shard_map/all_to_all | solution.py:19
  94.1 0.1 reduce_sum.56
  94.1 2.3 fusion.13
  96.4 0.0 copy-start.3
  96.4 0.0 copy-start.4
  96.4 0.0 all-reduce.4.cloned.1.call-update
  96.4 0.0 all-reduce.6.cloned.1.call-start
  96.5 149.2 %all-reduce.4.cloned.1.call-done = f32[512,1024]{1,0:T(8,128)} async-done(((f32[512,1024]{1,0:T(8,128)}), f32[512,1024]{1,0:T(8,128)}) %all-reduce.4.cloned.1.call-update) | async-done | bytes 2097168 | tf_op jit(solution)/shard_map/psum | solution.py:110
  245.6 0.0 all-reduce.6.cloned.1.call-update
  245.7 0.0 copy-done.3
  245.7 0.6 fusion.37
  248.9 0.1 add_reduce_fusion
  249.0 0.2 fusion.12
  249.2 31.9 %psum.30 = f32[512]{0:T(512)S(1)} all-reduce(f32[512]{0:T(512)S(1)} %bitcast.38), channel_id=1, replica_groups=mesh['dp'=32,'clus'=16] {'clus'}, use_global_device_ids=true, to_apply=%region_7.8 | all-reduce | flops 512 | bytes 4096 | tf_op jit(solution)/shard_map/psum | solution.py:110
  281.2 65.4 %psum.31 = f32[512]{0:T(512)S(1)} all-reduce(f32[512]{0:T(512)S(1)} %psum.30), channel_id=1, replica_groups=mesh['dp'=32,'clus'=16] {'dp'}, use_global_device_ids=true, to_apply=%region_8.9 | all-reduce | flops 512 | bytes 4096 | tf_op jit(solution)/shard_map/psum | solution.py:110
  346.5 0.0 copy-done.4
  346.5 0.1 fusion.6
  346.7 180.2 %all-reduce.6.cloned.1.call-done = f32[512,1024]{1,0:T(8,128)} async-done(((f32[512,1024]{1,0:T(8,128)}), f32[512,1024]{1,0:T(8,128)}) %all-reduce.6.cloned.1.call-update) | async-done | bytes 2097168 | tf_op jit(solution)/shard_map/psum | solution.py:110
  526.8 0.0 copy-start.1
  526.8 2.7 fusion.38
  529.5 0.0 copy-done.1
  529.5 1.2 add_divide_fusion
  530.7 0.0 copy-start
  530.7 1.3 copy-done
  532.1 1.4 fusion.39
  533.5 1.1 broadcast_in_dim.11
  534.6 7.4 %all-to-all-start.3 = ((f32[16,16,1024]{2,1,0:T(8,128)}), f32[16,16,1024]{2,1,0:T(8,128)S(1)}, u32[]{:S(2)}, u32[]{:S(2)}) async-start(f32[16,16,1024]{2,1,0:T(8,128)} %broadcast_in_dim.11), calls=%async_computation.3 | async-start | bytes 2097152 | tf_op jit(solution)/shard_map/all_to_all | solution.py:41
  541.9 0.6 broadcast_add_fusion.1
  542.6 1.4 dynamic-slice_convert_fusion
  544.0 24.9 %all-to-all-done.3 = f32[16,16,1024]{2,1,0:T(8,128)S(1)} async-done(((f32[16,16,1024]{2,1,0:T(8,128)}), f32[16,16,1024]{2,1,0:T(8,128)S(1)}, u32[]{:S(2)}, u32[]{:S(2)}) %all-to-all-start.3) | async-done | bytes 1048608 | tf_op jit(solution)/shard_map/all_to_all | solution.py:41
  568.8 1.4 fusion.2
  570.2 0.0 copy-start.7
  570.2 0.6 multiply_reduce_fusion
  570.8 0.2 fusion.7
  571.0 0.6 multiply_divide_fusion
  571.6 0.0 copy-done.7
  (10 shorter events, 0.1 us)
Async XLA Ops:
  7.2 15.7 %copy-start.2 = (bf16[256,1024]{1,0:T(8,128)(2,1)S(1)}, bf16[256,1024]{1,0:T(8,128)(2,1)}, u32[]{:S(2)}) copy-start(bf16[256,1024]{1,0:T(8,128)(2,1)} %param.6) | copy-start | bytes 1572868
  13.8 16.2 %all-to-all-start = ((s32[16,1,32]{2,1,0:T(1,128)}), s32[16,1,32]{2,1,0:T(1,128)S(1)}, u32[]{:S(2)}, u32[]{:S(2)}) async-start(s32[16,1,32]{2,1,0:T(1,128)} %all_to_all.15), calls=%async_computation | async-start | bytes 16384 | tf_op jit(solution)/shard_map/all_to_all | solution.py:89
  25.7 9.2 %copy-start.5 = (s32[256]{0:T(256)S(1)}, s32[256]{0:T(256)}, u32[]{:S(2)}) copy-start(s32[256]{0:T(256)} %param.8) | copy-start | bytes 3076
  30.0 29.5 %all-to-all-start.1 = ((bf16[16,32,1024]{2,1,0:T(8,128)(2,1)}), bf16[16,32,1024]{2,1,0:T(8,128)(2,1)S(1)}, u32[]{:S(2)}, u32[]{:S(2)}) async-start(bf16[16,32,1024]{2,1,0:T(8,128)(2,1)} %bitcast), calls=%async_computation.1 | async-start | bytes 2097152 | tf_op jit(solution)/shard_map/all_to_all | solution.py:88
  60.7 6.3 %copy-start.6 = (s32[256]{0:T(256)S(1)}, s32[256]{0:T(256)}, u32[]{:S(2)}) copy-start(s32[256]{0:T(256)} %param.9) | copy-start | bytes 3076
  61.9 32.2 %all-to-all-start.2 = ((f32[16,16,1025]{2,1,0:T(8,128)}), f32[16,16,1025]{2,1,0:T(8,128)S(1)}, u32[]{:S(2)}, u32[]{:S(2)}) async-start(f32[16,16,1025]{2,1,0:T(8,128)} %pad_maximum_fusion), calls=%async_computation.2 | async-start | bytes 2359296 | tf_op jit(solution)/shard_map/all_to_all | solution.py:19
  67.0 178.6 %all-reduce.4.cloned.1.call-start = ((), (), s32[]{:S(2)}) async-start(), calls=%async_computation.4 | async-start | bytes 4194304 | tf_op jit(solution)/shard_map/psum | solution.py:110
  96.4 149.3 %copy-start.3 = (f32[4]{0:T(128)S(1)}, f32[4]{0:T(128)}, u32[]{:S(2)}) copy-start(f32[4]{0:T(128)} %param.11) | copy-start | bytes 52
  96.4 250.1 %copy-start.4 = (s32[512]{0:T(512)S(1)}, s32[512]{0:T(512)}, u32[]{:S(2)}) copy-start(s32[512]{0:T(512)} %param.10) | copy-start | bytes 6148
  96.4 430.4 %all-reduce.6.cloned.1.call-start = ((), (), s32[]{:S(2)}) async-start(), calls=%async_computation.5 | async-start | bytes 4194304 | tf_op jit(solution)/shard_map/psum | solution.py:110
  526.8 2.7 copy-start.1
  530.7 1.4 copy-start
  534.6 34.2 %all-to-all-start.3 = ((f32[16,16,1024]{2,1,0:T(8,128)}), f32[16,16,1024]{2,1,0:T(8,128)S(1)}, u32[]{:S(2)}, u32[]{:S(2)}) async-start(f32[16,16,1024]{2,1,0:T(8,128)} %broadcast_in_dim.11), calls=%async_computation.3 | async-start | bytes 2097152 | tf_op jit(solution)/shard_map/all_to_all | solution.py:41
  570.2 1.4 copy-start.7
Sparse Core Ops, SparseCore 0:
  96.5 149.0 all-reduce.3
  248.6 278.2 all-reduce.5
